TPU v7x, 32 devices: a whole 2x2x4 slice. The times are simulated.
32 devices in a mesh: gy: 8 (over z, x), gz: 4 (over y, core).
Axes of the slice: x: 2, y: 2, z: 4, core: 2. Of those that a mesh axis runs over, the one named last changes fastest.
Arguments:
- density_seed: int32 [8, 512, 512], P(None, 'gy', 'gz'), may hold values from 0 to 15
- heat_load: float32 [8, 8, 512, 512], P(None, None, 'gy', 'gz'), may hold values from 0.3 to 3
- source_mask: int32 [8, 512, 512], P(None, 'gy', 'gz'), may hold values from 0 to 1, as said below
- fixed_mask: int32 [8, 512, 512], P(None, 'gy', 'gz'), may hold values 0 or 1
Outputs:
- temperature: float32 [8, 8, 512, 512], P(None, None, 'gy', 'gz')
- sensitivity: float32 [8, 512, 512], P(None, 'gy', 'gz')
Inputs may be any that keep to these rules, and one draw needn't show every extreme that they name: `source_mask`: 1 marks a node with a heat source, 0 a node without.
All inputs are finite; a program needn't handle non-finite values. No bound on the sum of `fixed_mask` on one device may be relied on, other than what follows from the above.
Results may differ from a plain program's by a relative error of at most 0.0055.
Values sent between devices are 32-bit elements; how exact they have to be, the bound alone decides.
A program may use at most 128 MiB of HBM per device.

v0:
```python
import jax
import jax.numpy as jnp
from jax import lax
from jax.sharding import PartitionSpec as P

ITERS = 4


cond_floor = 0.01
filter_weights = (1.0, 2.0, 3.0, 4.0, 3.0, 2.0, 1.0)
unit_corners = tuple(
    ((first, second, third) for first in (0, 1) for second in (0, 1) for third in (0, 1))
)


def padded_2(block, sides, width):
    for axis, dim in sides:
        count = lax.axis_size(axis)
        forward = [(i, i + 1) for i in range(count - 1)]
        backward = [(target, source) for source, target in forward]
        low = lax.ppermute(
            lax.slice_in_dim(block, block.shape[dim] - width, None, axis=dim), axis, forward
        )
        high = lax.ppermute(lax.slice_in_dim(block, 0, width, axis=dim), axis, backward)
        block = jnp.concatenate([low, block, high], axis=dim)
    return block


def from_behind(value, axis, steps):
    count = lax.axis_size(axis)
    initial, last = (max(0, -steps), min(count, count - steps))
    return lax.ppermute(value, axis, [(source, source + steps) for source in range(initial, last)])


def coupling(count):
    if count == 0:
        return 1.0 / 3.0
    if count == 1:
        return 0.0
    return -1.0 / 12.0


def differ(corner, other):
    return sum((int(corner[place] != other[place]) for place in range(3)))


def cut_nodes(padded, offset, shape3):
    return padded[
        ...,
        1 + offset[0] : 1 + offset[0] + shape3[0],
        1 + offset[1] : 1 + offset[1] + shape3[1],
        1 + offset[2] : 1 + offset[2] + shape3[2],
    ]


def conduct(field_pad, cond_pad, shape3):
    result = jnp.zeros((field_pad.shape[0],) + shape3, jnp.float32)
    for corner in unit_corners:
        element = tuple((-value for value in corner))
        cond = cut_nodes(cond_pad, element, shape3)
        inner = jnp.zeros_like(result)
        for other in unit_corners:
            weight = coupling(differ(corner, other))
            if weight == 0.0:
                continue
            offset = tuple((element[place] + other[place] for place in range(3)))
            inner = inner + weight * cut_nodes(field_pad, offset, shape3)
        result = result + cond[None] * inner
    return result


def cond_total(cond_pad, shape3):
    total = jnp.zeros(shape3, jnp.float32)
    for corner in unit_corners:
        element = tuple((-value for value in corner))
        total = total + cut_nodes(cond_pad, element, shape3)
    return total


def energy(field_pad, shape3):
    result = jnp.zeros((field_pad.shape[0],) + shape3, jnp.float32)
    for corner in unit_corners:
        left = cut_nodes(field_pad, corner, shape3)
        for other in unit_corners:
            weight = coupling(differ(corner, other))
            if weight == 0.0:
                continue
            result = result + weight * left * cut_nodes(field_pad, other, shape3)
    return jnp.mean(result, axis=0)


def filter_mass(index, total):
    mass = jnp.zeros(index.shape, jnp.float32)
    for step in range(-3, 4):
        inside = ((index + step >= 0) & (index + step < total)).astype(jnp.float32)
        mass = mass + (4.0 - abs(step)) * inside
    return mass


def smooth(array, axis, count):
    result = filter_weights[0] * lax.slice_in_dim(array, 0, count, axis=axis)
    for step in range(1, 7):
        result = result + filter_weights[step] * lax.slice_in_dim(
            array, step, step + count, axis=axis
        )
    return result


def node_rims(vector):
    extended = padded_2(vector, (("gy", 2), ("gz", 3)), 1)
    return jnp.pad(extended, ((0, 0), (1, 1), (0, 0), (0, 0)))


def inner_sum(left, right):
    return jnp.sum(left * right, axis=(1, 2, 3))


def column(values):
    return values[:, None, None, None]


def lower_rims(conductivity):
    below_y = from_behind(conductivity[:, -1:, :], "gy", 1)
    grown = jnp.concatenate([below_y, conductivity], axis=1)
    below_z = from_behind(grown[:, :, -1:], "gz", 1)
    grown = jnp.concatenate([below_z, grown], axis=2)
    return jnp.pad(grown, ((1, 1), (0, 1), (0, 1)))


def on_device(density_seed, heat_load, source_mask, fixed_mask):
    shape3 = density_seed.shape
    planes, rows_y, rows_z = shape3
    density = (density_seed.astype(jnp.float32) + 1.0) / 16.0
    conductivity = cond_floor + (1.0 - cond_floor) * density**3
    free = 1.0 - fixed_mask.astype(jnp.float32)
    cond_pad = lower_rims(conductivity)
    diagonal = free * cond_total(cond_pad, shape3) / 3.0 + (1.0 - free)
    inverse = 1.0 / diagonal
    rhs = heat_load * (source_mask.astype(jnp.float32) * free)[None]
    solution = jnp.zeros_like(rhs)
    residual = rhs

    def search_total(residual_now, precond_now):
        return column(lax.psum(inner_sum(residual_now, precond_now), ("gy", "gz")))

    precond = residual * inverse[None]
    direction = precond
    search = search_total(residual, precond)
    for step in range(ITERS):
        padded = node_rims(direction * free[None])
        image = free[None] * conduct(padded, cond_pad, shape3) + (1.0 - free)[None] * direction
        alpha = search / column(lax.psum(inner_sum(direction, image), ("gy", "gz")))
        solution = solution + alpha * direction
        residual = residual - alpha * image
        precond = residual * inverse[None]
        search_next = search_total(residual, precond)
        direction = precond + search_next / search * direction
        search = search_next
    mean_energy = energy(node_rims(solution), shape3)
    raw = -3.0 * (1.0 - cond_floor) * density**2 * mean_energy
    index_x = jnp.arange(planes, dtype=jnp.int32)
    index_y = lax.axis_index("gy") * rows_y + jnp.arange(rows_y, dtype=jnp.int32)
    index_z = lax.axis_index("gz") * rows_z + jnp.arange(rows_z, dtype=jnp.int32)
    mass_x = filter_mass(index_x, planes)
    mass_y = filter_mass(index_y, rows_y * lax.axis_size("gy"))
    mass_z = filter_mass(index_z, rows_z * lax.axis_size("gz"))
    mass = mass_x[:, None, None] * mass_y[None, :, None] * mass_z[None, None, :]
    scaled = raw / mass
    extended = padded_2(scaled, (("gy", 1), ("gz", 2)), 3)
    extended = jnp.pad(extended, ((3, 3), (0, 0), (0, 0)))
    result = smooth(extended, 0, planes)
    result = smooth(result, 1, rows_y)
    result = smooth(result, 2, rows_z)
    return (solution, result)


def solution(mesh):
    in_specs = (
        P(None, "gy", "gz"),
        P(None, None, "gy", "gz"),
        P(None, "gy", "gz"),
        P(None, "gy", "gz"),
    )
    out_specs = (P(None, None, "gy", "gz"), P(None, "gy", "gz"))
    return jax.shard_map(
        on_device, mesh=mesh, in_specs=in_specs, out_specs=out_specs, check_vma=False
    )
```

profile of v0, /device:TPU:0, one launch (start us, length us, event | category | flops | bytes accessed | tf_op | source)
XLA Modules:
  0.0 716.2 jit_solution(9199028748953225091)
XLA Ops:
  1.7 4.8 collective-permute-start
  14.6 4.2 collective-permute-start.2
  20.4 4.7 collective-permute-done.3
  31.5 3.0 copy.75
  34.6 7.1 collective-permute-start.5
  53.2 3.0 copy.76
  56.1 10.1 %select_maximum_fusion.16 = f32[8,10,66,130]{3,1,2,0:T(8,128)} fusion(f32[8,8,66,1]{3,1,2,0:T(8,128)} %copy.74, f32[8,8,66,1]{3,1,2,0:T(8,128)} %copy.76, f32[8,8,1,128]{3,1,2,0:T(8,128)S(1)} %collective-permute-done.3, f32[8,8,64,128]{3,1,2,0:T(8,128)} %copy-done.6, f32[8,8,1,128]{3,1,2,0:T(8,128)S(1)} %collective-permute-done.2), kind=kLoop, calls=%fused_computation.18 | loop fusion | flops 8236800 | bytes 4942080 | tf_op jit(solution)/shard_map/concatenate | solution.py:25
  66.2 39.8 %fusion.3 = (f32[8]{0:T(128)S(1)}, f32[8]{0:T(128)S(1)}, f32[8,8,64,128]{3,1,2,0:T(8,128)}) fusion(f32[8,64,128]{2,0,1:T(8,128)S(1)} %copy.70, f32[8,64,128]{2,0,1:T(8,128)S(1)} %copy.68, f32[8,8,64,128]{3,2,1,0:T(8,128)S(1)} %copy-done, f32[8,64,128]{2,0,1:T(8,128)} %copy.86, f32[8,10,66,130]{3,1,2,0:T(8,128)} %select_maximum_fusion.16, ...), kind=kLoop, calls=%fused_computation.50 | loop fusion | flops 46661616 | bytes 43091008 | tf_op jit(solution)/shard_map/reduce_sum | solution.py:115
  106.0 43.8 %all-reduce.7 = (f32[8]{0:T(128)S(1)}, f32[8]{0:T(128)S(1)}) all-reduce(f32[8]{0:T(128)S(1)} %get-tuple-element.9, f32[8]{0:T(128)S(1)} %get-tuple-element.8), channel_id=1, replica_groups=mesh['gy'=8,'gz'=4] {'gy','gz'}, use_global_device_ids=true, to_apply=%region_1.2 | all-reduce | flops 16 | bytes 128 | tf_op jit(solution)/shard_map/psum | solution.py:144
  149.8 3.0 fusion.7
  152.9 39.1 %psum.58 = f32[8]{0:T(128)S(1)} all-reduce(f32[8]{0:T(128)S(1)} %fusion.7), channel_id=1, replica_groups=mesh['gy'=8,'gz'=4] {'gy','gz'}, use_global_device_ids=true, to_apply=%region_5.6 | all-reduce | flops 8 | bytes 64 | tf_op jit(solution)/shard_map/psum | solution.py:144
  191.9 4.7 broadcast_multiply_fusion.2
  196.6 4.2 collective-permute-start.6
  202.4 4.2 collective-permute-done.7
  213.1 3.0 copy.89
  216.2 3.6 collective-permute-start.9
  222.0 3.0 copy.90
  225.0 10.1 %select_maximum_fusion.12 = f32[8,10,66,130]{3,1,2,0:T(8,128)} fusion(f32[8,8,66,1]{3,1,2,0:T(8,128)} %copy.88, f32[8,8,66,1]{3,1,2,0:T(8,128)} %copy.90, f32[8,8,1,128]{3,1,2,0:T(8,128)S(1)} %collective-permute-done.7, f32[8,8,64,128]{3,1,2,0:T(8,128)} %copy-done.3, f32[8,8,1,128]{3,1,2,0:T(8,128)S(1)} %collective-permute-done.6), kind=kLoop, calls=%fused_computation.14 | loop fusion | flops 8236800 | bytes 4942080 | tf_op jit(solution)/shard_map/concatenate | solution.py:25
  235.1 39.6 %multiply_reduce_fusion.1 = (f32[8]{0:T(128)S(1)}, f32[8,8,64,128]{3,1,2,0:T(8,128)}) fusion(f32[8,8,64,128]{3,1,2,0:T(8,128)} %get-tuple-element.23, f32[8,64,128]{2,0,1:T(8,128)} %copy.86, f32[8,10,66,130]{3,1,2,0:T(8,128)} %select_maximum_fusion.12, f32[8,64,128]{2,0,1:T(8,128)} %copy.85, f32[8,64,128]{2,0,1:T(8,128)} %copy.84, f32[8,64,128]{2,0,1:T(8,128)} %copy.83, ...), kind=kLoop, calls=%fused_computation.397 | loop fusion | flops 44564472 | bytes 42566688 | tf_op jit(solution)/shard_map/reduce_sum | solution.py:115
  274.8 41.4 %psum.59 = f32[8]{0:T(128)S(1)} all-reduce(f32[8]{0:T(128)S(1)} %get-tuple-element.20), channel_id=1, replica_groups=mesh['gy'=8,'gz'=4] {'gy','gz'}, use_global_device_ids=true, to_apply=%region_7.8 | all-reduce | flops 8 | bytes 64 | tf_op jit(solution)/shard_map/psum | solution.py:152
  316.2 5.0 fusion.8
  321.2 38.7 %psum.60 = f32[8]{0:T(128)S(1)} all-reduce(f32[8]{0:T(128)S(1)} %get-tuple-element.18), channel_id=1, replica_groups=mesh['gy'=8,'gz'=4] {'gy','gz'}, use_global_device_ids=true, to_apply=%region_9.10 | all-reduce | flops 8 | bytes 64 | tf_op jit(solution)/shard_map/psum | solution.py:144
  359.9 4.0 broadcast_multiply_fusion.1
  364.0 4.2 collective-permute-start.10
  369.8 4.2 collective-permute-done.11
  380.5 3.0 copy.95
  383.6 3.6 collective-permute-start.13
  389.4 3.0 copy.96
  392.4 10.1 %select_maximum_fusion.8 = f32[8,10,66,130]{3,1,2,0:T(8,128)} fusion(f32[8,8,66,1]{3,1,2,0:T(8,128)} %copy.94, f32[8,8,66,1]{3,1,2,0:T(8,128)} %copy.96, f32[8,8,1,128]{3,1,2,0:T(8,128)S(1)} %collective-permute-done.11, f32[8,8,64,128]{3,1,2,0:T(8,128)} %copy-done.4, f32[8,8,1,128]{3,1,2,0:T(8,128)S(1)} %collective-permute-done.10), kind=kLoop, calls=%fused_computation.10 | loop fusion | flops 8236800 | bytes 4942080 | tf_op jit(solution)/shard_map/concatenate | solution.py:25
  402.5 39.7 %multiply_reduce_fusion = (f32[8]{0:T(128)S(1)}, f32[8,8,64,128]{3,1,2,0:T(8,128)}) fusion(f32[8,8,64,128]{3,1,2,0:T(8,128)} %get-tuple-element.17, f32[8,64,128]{2,0,1:T(8,128)} %copy.86, f32[8,10,66,130]{3,1,2,0:T(8,128)} %select_maximum_fusion.8, f32[8,64,128]{2,0,1:T(8,128)} %copy.85, f32[8,64,128]{2,0,1:T(8,128)} %copy.84, f32[8,64,128]{2,0,1:T(8,128)} %copy.83, ...), kind=kLoop, calls=%fused_computation.390 | loop fusion | flops 44564472 | bytes 42566688 | tf_op jit(solution)/shard_map/reduce_sum | solution.py:115
  442.2 41.3 %psum.61 = f32[8]{0:T(128)S(1)} all-reduce(f32[8]{0:T(128)S(1)} %get-tuple-element.14), channel_id=1, replica_groups=mesh['gy'=8,'gz'=4] {'gy','gz'}, use_global_device_ids=true, to_apply=%region_11.12 | all-reduce | flops 8 | bytes 64 | tf_op jit(solution)/shard_map/psum | solution.py:152
  486.2 38.9 %psum.62 = f32[8]{0:T(128)S(1)} all-reduce(f32[8]{0:T(128)S(1)} %fusion.9), channel_id=1, replica_groups=mesh['gy'=8,'gz'=4] {'gy','gz'}, use_global_device_ids=true, to_apply=%region_13.14 | all-reduce | flops 8 | bytes 64 | tf_op jit(solution)/shard_map/psum | solution.py:144
  525.1 4.7 broadcast_multiply_fusion
  529.8 4.2 collective-permute-start.14
  535.6 4.2 collective-permute-done.15
  546.3 3.0 copy.101
  549.4 4.0 collective-permute-start.17
  558.7 10.1 %select_maximum_fusion.4 = f32[8,10,66,130]{3,1,2,0:T(8,128)} fusion(f32[8,8,66,1]{3,1,2,0:T(8,128)} %copy.100, f32[8,8,66,1]{3,1,2,0:T(8,128)} %copy.102, f32[8,8,1,128]{3,1,2,0:T(8,128)S(1)} %collective-permute-done.15, f32[8,8,64,128]{3,1,2,0:T(8,128)} %copy-done.5, f32[8,8,1,128]{3,1,2,0:T(8,128)S(1)} %collective-permute-done.14), kind=kLoop, calls=%fused_computation.6 | loop fusion | flops 8236800 | bytes 4942080 | tf_op jit(solution)/shard_map/concatenate | solution.py:25
  568.8 39.3 %fusion.234 = f32[8]{0:T(128)S(1)} fusion(f32[8,8,64,128]{3,1,2,0:T(8,128)} %get-tuple-element.13, f32[8,10,66,130]{3,1,2,0:T(8,128)} %select_maximum_fusion.4, f32[8,8,1,128]{3,1,2,0:T(8,128)S(1)} %collective-permute-done.15, f32[8,8,64,128]{3,1,2,0:T(8,128)} %copy-done.5, f32[8,8,1,128]{3,1,2,0:T(8,128)S(1)} %collective-permute-done.14, ...), kind=kLoop, calls=%fused_computation.410 | loop fusion | flops 44564472 | bytes 40469536 | tf_op jit(solution)/shard_map/reduce_sum | solution.py:115
  608.1 39.9 %psum.63 = f32[8]{0:T(128)S(1)} all-reduce(f32[8]{0:T(128)S(1)} %fusion.234), channel_id=1, replica_groups=mesh['gy'=8,'gz'=4] {'gy','gz'}, use_global_device_ids=true, to_apply=%region_15.16 | all-reduce | flops 8 | bytes 64 | tf_op jit(solution)/shard_map/psum | solution.py:152
  648.0 4.9 fusion.6
  654.2 4.2 collective-permute-start.18
  660.0 4.2 collective-permute-done.19
  672.5 3.2 collective-permute-start.21
  680.1 7.0 select_maximum_fusion
  687.2 9.9 %fusion.233 = f32[8,64,128]{2,0,1:T(8,128)S(1)} fusion(f32[8,8,64,128]{3,1,2,0:T(8,128)S(1)} %copy-done.2, f32[8,10,66,130]{3,1,2,0:T(8,128)S(1)} %select_maximum_fusion, f32[8,8,1,128]{3,1,2,0:T(8,128)S(1)} %collective-permute-done.19, f32[8,8,66,1]{3,1,2,0:T(8,128)S(1)} %copy-done.7, f32[8,8,1,128]{3,1,2,0:T(8,128)S(1)} %collective-permute-done.18), kind=kLoop, calls=%fused_computation.409 | loop fusion | flops 53936128 | bytes 10830336 | tf_op jit(solution)/shard_map/reduce_sum | solution.py:89
  697.3 3.2 collective-permute-start.22
  701.9 4.2 collective-permute-done.23
  (141 shorter events, 92.4 us)
Async XLA Ops:
  0.6 10.2 %copy-start.15 = (s32[8,64,128]{2,1,0:T(8,128)S(1)}, s32[8,64,128]{2,1,0:T(8,128)}, u32[]{:S(2)}) copy-start(s32[8,64,128]{2,1,0:T(8,128)} %param.6) | copy-start | bytes 786436
  0.6 10.2 %copy-start.14 = (s32[8,64,128]{2,1,0:T(8,128)S(1)}, s32[8,64,128]{2,1,0:T(8,128)}, u32[]{:S(2)}) copy-start(s32[8,64,128]{2,1,0:T(8,128)} %param.7) | copy-start | bytes 786436
  1.7 6.2 collective-permute-start
  8.1 2.5 collective-permute-start.1
  10.8 2.3 copy-start
  14.6 10.5 %copy-start.6 = (f32[8,8,64,128]{3,1,2,0:T(8,128)}, f32[8,8,64,128]{3,1,2,0:T(8,128)S(1)}, u32[]{:S(2)}) copy-start(f32[8,8,64,128]{3,1,2,0:T(8,128)S(1)} %multiply_multiply_fusion.15) | copy-start | bytes 6291460
  14.6 5.8 collective-permute-start.2
  18.8 6.2 collective-permute-start.3
  30.2 20.7 %collective-permute-start.4 = (f32[8,8,66,1]{2,1,3,0:T(8,128)S(1)}, f32[8,8,66,1]{2,1,3,0:T(8,128)S(1)}, u32[]{:S(2)}, u32[]{:S(2)}) collective-permute-start(f32[8,8,66,1]{2,1,3,0:T(8,128)S(1)} %copy.73), channel_id=1, source_target_pairs={{1,0},{2,1},{3,2},{5,4},{6,5},{7,6},{9,8},{10,9},{11,10},{13,12},{... | collective-permute-start | bytes 50696 | tf_op jit(solution)/shard_map/ppermute | solution.py:24
  34.6 12.0 %copy-start.13 = (f32[8,64,128]{2,1,0:T(8,128)S(1)}, f32[8,64,128]{2,1,0:T(8,128)}, u32[]{:S(2)}) copy-start(f32[8,64,128]{2,1,0:T(8,128)} %get-tuple-element.50) | copy-start | bytes 786436
  34.6 12.9 %copy-start.12 = (f32[8,64,128]{2,1,0:T(8,128)S(1)}, f32[8,64,128]{2,1,0:T(8,128)}, u32[]{:S(2)}) copy-start(f32[8,64,128]{2,1,0:T(8,128)} %get-tuple-element.47) | copy-start | bytes 786436
  34.6 13.8 %copy-start.11 = (f32[8,64,128]{2,1,0:T(8,128)S(1)}, f32[8,64,128]{2,1,0:T(8,128)}, u32[]{:S(2)}) copy-start(f32[8,64,128]{2,1,0:T(8,128)} %get-tuple-element.48) | copy-start | bytes 786436
  34.6 14.6 %copy-start.10 = (f32[8,64,128]{2,1,0:T(8,128)S(1)}, f32[8,64,128]{2,1,0:T(8,128)}, u32[]{:S(2)}) copy-start(f32[8,64,128]{2,1,0:T(8,128)} %get-tuple-element.49) | copy-start | bytes 786436
  34.6 15.5 %copy-start.9 = (f32[8,64,128]{2,1,0:T(8,128)S(1)}, f32[8,64,128]{2,1,0:T(8,128)}, u32[]{:S(2)}) copy-start(f32[8,64,128]{2,1,0:T(8,128)} %get-tuple-element.55) | copy-start | bytes 786436
  34.6 18.6 %collective-permute-start.5 = (f32[8,8,66,1]{2,1,3,0:T(8,128)}, f32[8,8,66,1]{2,1,3,0:T(8,128)}, u32[]{:S(2)}, u32[]{:S(2)}) collective-permute-start(f32[8,8,66,1]{2,1,3,0:T(8,128)} %copy.75), channel_id=1, source_target_pairs={{0,1},{1,2},{2,3},{4,5},{5,6},{6,7},{8,9},{9,10},{10,11},{12,13},{... | collective-permute-start | bytes 50696 | tf_op jit(solution)/shard_map/ppermute | solution.py:21
  196.6 10.2 %copy-start.3 = (f32[8,8,64,128]{3,1,2,0:T(8,128)}, f32[8,8,64,128]{3,1,2,0:T(8,128)S(1)}, u32[]{:S(2)}) copy-start(f32[8,8,64,128]{3,1,2,0:T(8,128)S(1)} %get-tuple-element.22) | copy-start | bytes 6291460
  196.6 5.8 collective-permute-start.6
  200.8 5.8 collective-permute-start.7
  211.8 8.0 %collective-permute-start.8 = (f32[8,8,66,1]{2,1,3,0:T(8,128)S(1)}, f32[8,8,66,1]{2,1,3,0:T(8,128)S(1)}, u32[]{:S(2)}, u32[]{:S(2)}) collective-permute-start(f32[8,8,66,1]{2,1,3,0:T(8,128)S(1)} %copy.87), channel_id=1, source_target_pairs={{1,0},{2,1},{3,2},{5,4},{6,5},{7,6},{9,8},{10,9},{11,10},{13,12},{... | collective-permute-start | bytes 50696 | tf_op jit(solution)/shard_map/ppermute | solution.py:24
  216.2 5.9 collective-permute-start.9
  359.9 4.1 copy-start.18
  364.0 10.2 %copy-start.4 = (f32[8,8,64,128]{3,1,2,0:T(8,128)}, f32[8,8,64,128]{3,1,2,0:T(8,128)S(1)}, u32[]{:S(2)}) copy-start(f32[8,8,64,128]{3,1,2,0:T(8,128)S(1)} %get-tuple-element.16) | copy-start | bytes 6291460
  364.0 5.8 collective-permute-start.10
  368.2 5.8 collective-permute-start.11
  379.2 8.0 %collective-permute-start.12 = (f32[8,8,66,1]{2,1,3,0:T(8,128)S(1)}, f32[8,8,66,1]{2,1,3,0:T(8,128)S(1)}, u32[]{:S(2)}, u32[]{:S(2)}) collective-permute-start(f32[8,8,66,1]{2,1,3,0:T(8,128)S(1)} %copy.93), channel_id=1, source_target_pairs={{1,0},{2,1},{3,2},{5,4},{6,5},{7,6},{9,8},{10,9},{11,10},{13,12},{... | collective-permute-start | bytes 50696 | tf_op jit(solution)/shard_map/ppermute | solution.py:24
  383.6 5.9 collective-permute-start.13
  402.5 81.0 %copy-start.19 = (f32[8]{0:T(128)S(1)}, f32[8]{0:T(128)}, u32[]{:S(2)}) copy-start(f32[8]{0:T(128)} %copy-done.18) | copy-start | bytes 100
  525.1 4.7 copy-start.16
  529.8 10.2 %copy-start.5 = (f32[8,8,64,128]{3,1,2,0:T(8,128)}, f32[8,8,64,128]{3,1,2,0:T(8,128)S(1)}, u32[]{:S(2)}) copy-start(f32[8,8,64,128]{3,1,2,0:T(8,128)S(1)} %get-tuple-element.12) | copy-start | bytes 6291460
  529.8 5.8 collective-permute-start.14
  534.0 5.8 collective-permute-start.15
  545.0 8.4 %collective-permute-start.16 = (f32[8,8,66,1]{2,1,3,0:T(8,128)S(1)}, f32[8,8,66,1]{2,1,3,0:T(8,128)S(1)}, u32[]{:S(2)}, u32[]{:S(2)}) collective-permute-start(f32[8,8,66,1]{2,1,3,0:T(8,128)S(1)} %copy.99), channel_id=1, source_target_pairs={{1,0},{2,1},{3,2},{5,4},{6,5},{7,6},{9,8},{10,9},{11,10},{13,12},{... | collective-permute-start | bytes 50696 | tf_op jit(solution)/shard_map/ppermute | solution.py:24
  549.4 6.3 collective-permute-start.17
  568.8 79.3 %copy-start.17 = (f32[8]{0:T(128)S(1)}, f32[8]{0:T(128)}, u32[]{:S(2)}) copy-start(f32[8]{0:T(128)} %copy-done.16) | copy-start | bytes 100
  652.9 1.3 copy-start.1
  654.2 5.8 collective-permute-start.18
  658.4 5.8 collective-permute-start.19
  670.4 5.4 collective-permute-start.20
  672.5 5.5 collective-permute-start.21
  675.8 4.4 copy-start.2
  680.1 7.0 copy-start.7
  687.2 9.9 %copy-start.8 = (s32[8,64,128]{2,1,0:T(8,128)S(1)}, s32[8,64,128]{2,1,0:T(8,128)}, u32[]{:S(2)}) copy-start(s32[8,64,128]{2,1,0:T(8,128)} %param.4) | copy-start | bytes 786436
  697.3 4.6 collective-permute-start.22
  700.4 5.6 collective-permute-start.23
  706.2 5.4 collective-permute-start.24
  708.6 5.3 collective-permute-start.25
where the time goes:
time: 727 us; the launch traced here: 716 us
  blocking collectives  283 us (39%)
  other arithmetic  254 us (35%)
  local copies, waits for them, and re-layouts  76.2 us (10%)
  starting transfers between devices  69.7 us (10%)
  waiting for transfers between devices  32.1 us (4%)
    reduce_sum x7, other arithmetic, inner_sum(): return jnp.sum(left * right, axis=(1, 2, 3))  169 us
    psum x4, blocking collectives, search_total(): return column(lax.psum(inner_sum(residual_now, precond_now), ('gy', 'gz')))  160 us
    psum x3, blocking collectives, on_device(): alpha = search / column(lax.psum(inner_sum(direction, image), ('gy', 'gz')))  123 us
    concatenate x12, other arithmetic, padded_2(): block = jnp.concatenate([low, block, high], axis=dim)  50 us
    ppermute x12, starting transfers between devices, padded_2(): lax.ppermute(lax.slice_in_dim(block, block.shape[dim] - width, None, axis...  48 us
    ppermute x12, waiting for transfers between devices, padded_2(): lax.ppermute(lax.slice_in_dim(block, 0, width, axis=dim), axis, backward)  28.1 us
    slice x17, local copies, waits for them, and re-layouts, padded_2(): lax.slice_in_dim(block, block.shape[dim] - width, None, axis=dim)  25.8 us
    ppermute x12, starting transfers between devices, padded_2(): lax.ppermute(lax.slice_in_dim(block, 0, width, axis=dim), axis, backward)  15.5 us
  transfers between devices with their start and end apart: 26, of which 15 were waited for; matrix products, arithmetic and copies ran while one was open for 5% of the time, Pallas kernels for 0%

commit v1 on v0

v1 whole, which is shorter than its diff:
```python
import functools

import jax
import jax.numpy as jnp
from jax import lax
from jax.experimental import pallas as pl
from jax.experimental.pallas import tpu as pltpu
from jax.sharding import PartitionSpec as P

STEPS = 4
L, X = 8, 8
R, Z = 64, 128
LO, HI, RP = 8, 72, 80
MESH = pl.DeviceIdType.MESH
FLOOR = 0.01
HALF = 0.75

NEAR = ((1, 0), (-1, 0), (0, 1), (0, -1), (1, 1), (1, -1), (-1, 1), (-1, -1))


def roll(v, shift):
    if isinstance(shift, int):
        shift = shift % 128
        if shift == 0:
            return v
    return pltpu.roll(v, shift, v.ndim - 1)


def kernel(ny, nz, seed, heat, source, fixed, temp, sens,
           U, BL, BO, BH, ELO, EHI, ETOP, EBOT, W, WC,
           C1, C2, C3, INV, DIAG, PS, ACC, RED, COEF,
           BC, BCL, CTOP, CLO, S, SLO, SHI, PZ, PZL, PZH, PM,
           AZ, AY, send, recv, rsend, rrecv):
    my_y, my_z = lax.axis_index("gy"), lax.axis_index("gz")
    f32 = jnp.float32
    lane = lax.broadcasted_iota(jnp.int32, (8, Z), 1)
    sub = lax.broadcasted_iota(jnp.int32, (8, Z), 0)
    lane16 = lax.rem(lane, 16)
    group = lax.div(lane, 16)
    zero = jnp.zeros((8, Z), f32)
    chunks = tuple(range(LO, HI, 8))

    def inside(dy, dz):
        ok = None
        for d, me, n in ((dy, my_y, ny), (dz, my_z, nz)):
            if d:
                this = (me + d >= 0) & (me + d < n)
                ok = this if ok is None else ok & this
        return ok

    for ref in (BL, BO, BH):
        ref[...] = jnp.zeros(ref.shape, f32)
    for ref in (ELO, EHI, BCL, CLO, SLO, SHI, PZL, PZH, C1, C2, C3, W):
        ref[...] = jnp.zeros(ref.shape, f32)

    barrier = pltpu.get_barrier_semaphore()
    for d in range(1, nz):
        pl.semaphore_signal(barrier, inc=1, device_id=(my_y, lax.rem(my_z + d, nz)), device_id_type=MESH)
    for d in range(1, ny):
        pl.semaphore_signal(barrier, inc=1, device_id=(lax.rem(my_y + d, ny), my_z), device_id_type=MESH)
    for dy, dz in NEAR[4:]:
        @pl.when(inside(dy, dz))
        def _(dy=dy, dz=dz):
            pl.semaphore_signal(barrier, inc=1, device_id=(my_y + dy, my_z + dz), device_id_type=MESH)

    for x in range(X):
        for r in range(0, R, 8):
            density = (seed[x, r:r + 8, :].astype(f32) + 1.0) / 16.0
            cond = (FLOOR + (1.0 - FLOOR) * (density * density * density)) * (1.0 / 48.0)
            C1[x, LO + r:LO + r + 8, :] = cond * 3.0
            C2[x, LO + r:LO + r + 8, :] = cond * 2.0
            C3[x, LO + r:LO + r + 8, :] = cond
            if r == R - 8:
                CTOP[x:x + 1, :] = cond[7:8, :]
    for r in range(LO, HI, 8):
        b = zero
        for x in range(X):
            b = jnp.where(lane16 >= 2 * x, roll(C3[x, r:r + 8, :], 2 * x + 1), b)
        b = jnp.where(group == 0, b, 0.0)
        for s in (16, 32, 64):
            b = b + roll(b, s)
        BC[r - LO:r - LO + 8, :] = b

    def sides(me, n):
        return jnp.where(me > 0, 1, 0) + jnp.where(me + 1 < n, 1, 0)

    pl.semaphore_wait(barrier, nz - 1 + ny - 1 + sides(my_y, ny) * sides(my_z, nz))

    def exchange(e, messages, start):
        for i, (dy, dz, src, dst) in enumerate(messages):
            def copy(dy=dy, dz=dz, src=src, dst=dst, i=i):
                return pltpu.make_async_remote_copy(
                    src_ref=src, dst_ref=dst, send_sem=send.at[e, i], recv_sem=recv.at[e, i],
                    device_id=(my_y + dy, my_z + dz), device_id_type=MESH)
            if start:
                @pl.when(inside(dy, dz))
                def _(copy=copy):
                    copy().start()
            else:
                @pl.when(inside(dy, dz))
                def _(copy=copy):
                    copy().wait_send()
                @pl.when(inside(-dy, -dz))
                def _(copy=copy):
                    copy().wait_recv()

    low, high = pl.ds(0, 8), pl.ds(HI, 8)
    first, last, mid = pl.ds(LO, 8), pl.ds(HI - 8, 8), pl.ds(LO, R)

    def halo(j):
        own = BO.at[j]
        return (
            (1, 0, ETOP.at[j], ELO.at[j]), (-1, 0, EBOT.at[j], EHI.at[j]),
            (0, 1, own.at[mid], BL.at[j].at[mid]), (0, -1, own.at[mid], BH.at[j].at[mid]),
            (1, 0, own.at[last], BO.at[j].at[low]), (-1, 0, own.at[first], BO.at[j].at[high]),
            (1, 1, own.at[last], BL.at[j].at[low]), (1, -1, own.at[last], BH.at[j].at[low]),
            (-1, 1, own.at[first], BL.at[j].at[high]), (-1, -1, own.at[first], BH.at[j].at[high]),
        )

    cond_messages = (
        (1, 0, CTOP, CLO),
        (0, 1, BC, BCL.at[mid]),
        (1, 1, BC.at[pl.ds(R - 8, 8)], BCL.at[low]),
    )
    exchange(STEPS, cond_messages, True)
    exchange(STEPS, cond_messages, False)
    for x in range(X):
        for ref, k in ((C1, 3.0), (C2, 2.0), (C3, 1.0)):
            ref[x, LO - 1:LO, :] = CLO[x:x + 1, :] * k

    for r in chunks:
        low_z = BCL[r:r + 8, :] + BCL[r - 1:r + 7, :]
        low_z = low_z + jnp.where(lane16 >= 2, roll(low_z, 2), 0.0)
        before = None
        for x in range(X):
            t = C3[x, r:r + 8, :] + C3[x, r - 1:r + 7, :]
            both = t if before is None else t + before
            before = t
            below = jnp.where(lane == 0, roll(low_z, -2 * x), roll(both, 1))
            total = (both + below) * 48.0 / 3.0
            free = 1.0 - fixed[x, r - LO:r - LO + 8, :].astype(f32)
            DIAG[x, r - LO:r - LO + 8, :] = total
            INV[x, r - LO:r - LO + 8, :] = free / total

    def pack_tail(j, l, r, b):
        BO[j, r:r + 8, :] = jnp.where(group == l, b, BO[j, r:r + 8, :])

    def edges(j, l, x, r, v):
        if r == LO:
            EBOT[j, l, x:x + 1, :] = v[0:1, :]
        if r == HI - 8:
            ETOP[j, l, x:x + 1, :] = v[7:8, :]

    @pl.loop(0, L)
    def _(l):
        acc = zero
        for r in chunks:
            b = zero
            q = r - LO
            for x in range(X):
                inv = INV[x, q:q + 8, :]
                rhs = heat[l, x, q:q + 8, :] * source[x, q:q + 8, :].astype(f32)
                v = rhs * inv
                U[0, l, x, r:r + 8, :] = v
                acc = acc + v * v * DIAG[x, q:q + 8, :]
                b = jnp.where(lane16 >= 2 * x, roll(v, 16 * l + 2 * x + 1), b)
                edges(0, l, x, r, v)
            pack_tail(0, l, r, b)
        ACC[0, l] = acc
    exchange(0, halo(0), True)

    def fill(j):
        @pl.loop(0, L)
        def _(l):
            for x in range(X):
                U[j, l, x, LO - 1:LO, :] = ELO[j, l, x:x + 1, :]
                U[j, l, x, HI:HI + 1, :] = EHI[j, l, x:x + 1, :]

        def up_x(v):
            return jnp.where(lane16 < 14, roll(v, -2), 0.0)

        def down_x(v):
            return jnp.where(lane16 >= 2, roll(v, 2), 0.0)

        for r in (0,) + chunks:
            a0, a1 = BL[j, r:r + 8, :], BL[j, r + 1:r + 9, :]
            b0, b1 = roll(BO[j, r:r + 8, :], -1), roll(BO[j, r + 1:r + 9, :], -1)
            c = BCL[r:r + 8, :]
            pushes = []
            s0, d0, s1, d1 = a0 + b0, b0 - a0, a1 + b1, b1 - a1
            fields = ((s0 + s1, 0), (s1 - s0, 1), (d0 + d1, 1), (d1 - d0, 2))
            outs = []
            for f, k in fields:
                g = up_x(f)
                td = (g - f) * (c * float(3 - k))
                ts = None if k == 0 else (f + g) * (c * float(4 - k))
                if ts is None:
                    outs.append(down_x(td) - td)
                else:
                    outs.append(ts - td + down_x(ts + td))
            ss, sd, ds, dd = outs
            ps, pd = ss + ds, sd + dd
            WC[0, r:r + 8, :] = ps + pd
            if r:
                push = ps - pd + WC[0, r - 1:r + 7, :]
                push = roll(push, 1)
            else:
                push = zero
            W[j, r:r + 8, :] = jnp.where(lax.rem(lane, 2) == 0, roll(BH[j, r:r + 8, :], -1), push)
        W[j, HI:RP, :] = roll(BH[j, HI:RP, :], -1)

    def step(j):
        scale = 2.0 if j else 1.0

        @pl.loop(0, L)
        def _(l):
            back = 128 - (16 * l + 1)
            acc_a, acc_b = zero, zero
            for r in (0,) + chunks:
                w0, w1 = W[j, r:r + 8, :], W[j, r + 1:r + 9, :]
                ws, wd = w0 + w1, w1 - w0
                b = zero
                carry = None
                last_f = None

                def node(x):
                    u0, u1 = U[j, l, x, r:r + 8, :], U[j, l, x, r + 1:r + 9, :]
                    amount = back - 2 * x
                    ys, yd = u0 + u1, u1 - u0
                    ns = jnp.where(lane == 127, roll(ws, amount), roll(ys, 127))
                    nd = jnp.where(lane == 127, roll(wd, amount), roll(yd, 127))
                    return (ys + ns, yd + nd, ns - ys, nd - yd)

                now = node(0)
                for x in range(X):
                    nxt = node(x + 1) if x + 1 < X else None
                    cs = (C1[x, r:r + 8, :], C2[x, r:r + 8, :], C3[x, r:r + 8, :])
                    outs, new_carry = [], []
                    for i, k in enumerate((0, 1, 1, 2)):
                        f = now[i]
                        if nxt is None:
                            d, s = -f, f
                        else:
                            d, s = nxt[i] - f, nxt[i] + f
                        td = d * cs[k]
                        if k == 0:
                            o, n = -td, td
                        else:
                            ts = s * cs[k - 1]
                            o, n = ts - td, ts + td
                        if carry is not None:
                            o = o + carry[i]
                        outs.append(o)
                        new_carry.append(n)
                    carry = new_carry
                    now = nxt
                    ss, sd, ds, dd = outs
                    PS[0, x, r:r + 8, :] = ss + sd
                    PS[1, x, r:r + 8, :] = ds + dd
                    if r == 0:
                        continue
                    q = r - LO
                    es = ss - sd + PS[0, x, r - 1:r + 7, :]
                    ed = ds - dd + PS[1, x, r - 1:r + 7, :]
                    push = jnp.where(lane == 0, roll(w0, back - 2 * x), roll(es + ed, 1))
                    image = es - ed + push
                    v = U[j, l, x, r:r + 8, :]
                    new = image * (INV[x, q:q + 8, :] * (scale / HALF)) - scale * v
                    if j:
                        new = new - U[j - 1, l, x, r:r + 8, :]
                    weighted = new * DIAG[x, q:q + 8, :]
                    acc_a = acc_a + v * weighted
                    if j + 1 < STEPS:
                        acc_b = acc_b + new * weighted
                        U[j + 1, l, x, r:r + 8, :] = new
                        b = jnp.where(lane16 >= 2 * x, roll(new, 16 * l + 2 * x + 1), b)
                        edges(j + 1, l, x, r, new)
                if r and j + 1 < STEPS:
                    pack_tail(j + 1, l, r, b)
            ACC[2 * j + 1, l] = acc_a
            if j + 1 < STEPS:
                ACC[2 * j + 2, l] = acc_b

    for j in range(STEPS):
        exchange(j, halo(j), False)
        fill(j)
        step(j)
        if j + 1 < STEPS:
            exchange(j + 1, halo(j + 1), True)

    rows = zero
    for k in range(2 * STEPS):
        for l in range(L):
            t = jnp.sum(jnp.sum(ACC[k, l], axis=0, keepdims=True), axis=1, keepdims=True)
            rows = jnp.where((sub == k) & (lane == l), t, rows)

    def spread(buffer, n, axis_z, base):
        def copy(d):
            target = (my_y, lax.rem(my_z + d, nz)) if axis_z else (lax.rem(my_y + d, ny), my_z)
            return pltpu.make_async_remote_copy(
                src_ref=buffer.at[0], dst_ref=buffer.at[d], send_sem=rsend.at[base + d],
                recv_sem=rrecv.at[base + d], device_id=target, device_id_type=MESH)
        for d in range(1, n):
            copy(d).start()
        for d in range(1, n):
            copy(d).wait()
        total = buffer[0]
        for d in range(1, n):
            total = total + buffer[d]
        return total

    AZ[0] = rows
    AY[0] = spread(AZ, nz, True, 0)
    RED[...] = spread(AY, ny, False, nz)
    a = [RED[k:k + 1, :] for k in range(2 * STEPS)]
    m = [a[0], a[1]]
    for k in range(2, 2 * STEPS):
        m.append(2.0 * a[k] - m[k % 2])

    def gram(i, j):
        return 0.5 * (m[i + j] + m[abs(i - j)])

    def times_m(c):
        out = [None] * (len(c) + 1)
        def put(i, v):
            out[i] = v if out[i] is None else out[i] + v
        for i, v in enumerate(c):
            put(i, HALF * v)
            put(i + 1, (HALF if i == 0 else 0.5 * HALF) * v)
            if i:
                put(i - 1, 0.5 * HALF * v)
        return out

    def form(c, e):
        total = 0.0
        for i, v in enumerate(c):
            for k, w in enumerate(e):
                total = total + v * w * gram(i, k)
        return total

    one = jnp.ones((1, Z), f32)
    zc, dc, tc = [one], [one], []
    rz = form(zc, zc)
    for it in range(STEPS):
        image = times_m(dc)
        alpha = rz / form(dc, image)
        tc = [alpha * v + (tc[i] if i < len(tc) else 0.0) for i, v in enumerate(dc)]
        if it + 1 == STEPS:
            break
        zc = [(zc[i] if i < len(zc) else 0.0) - alpha * v for i, v in enumerate(image)]
        new = form(zc, zc)
        beta = new / rz
        dc = [v + (beta * dc[i] if i < len(dc) else 0.0) for i, v in enumerate(zc)]
        rz = new

    packed = [zero] * STEPS
    for i in range(STEPS):
        for l in range(L):
            t = jnp.sum(jnp.where(lane[0:1] == l, tc[i], 0.0), axis=1, keepdims=True)
            t = jnp.broadcast_to(t, (8, Z))
            COEF[i, l] = t
            packed[i] = jnp.where(group == l, t, packed[i])
    for r in chunks + (HI,):
        WC[0, r:r + 8, :] = sum(packed[i] * W[i, r:r + 8, :] for i in range(1, STEPS)) + packed[0] * W[0, r:r + 8, :]

    S[...] = jnp.zeros(S.shape, f32)

    @pl.loop(0, L)
    def _(l):
        cs = [COEF[i, l] for i in range(STEPS)]
        back = 128 - (16 * l + 1)
        for x in range(X):
            for r in chunks + (HI,):
                t = cs[0] * U[0, l, x, r:r + 8, :]
                for i in range(1, STEPS):
                    t = t + cs[i] * U[i, l, x, r:r + 8, :]
                PS[0, x, r:r + 8, :] = t
                if r < HI:
                    temp[l, x, r - LO:r - LO + 8, :] = t
        for r in chunks:
            w0, w1 = WC[0, r:r + 8, :], WC[0, r + 1:r + 9, :]
            ws, wd = w0 + w1, w1 - w0

            def node(x):
                u0, u1 = PS[0, x, r:r + 8, :], PS[0, x, r + 1:r + 9, :]
                amount = back - 2 * x
                ys, yd = u0 + u1, u1 - u0
                ns = jnp.where(lane == 127, roll(ws, amount), roll(ys, 127))
                nd = jnp.where(lane == 127, roll(wd, amount), roll(yd, 127))
                return (ys + ns, yd + nd, ns - ys, nd - yd)

            now = node(0)
            for x in range(X):
                nxt = node(x + 1) if x + 1 < X else (zero,) * 4
                groups = [None, None, None]
                for i, k in enumerate((0, 1, 1, 2)):
                    d = nxt[i] - now[i]
                    groups[k] = d * d if groups[k] is None else groups[k] + d * d
                    if k:
                        s = nxt[i] + now[i]
                        groups[k - 1] = groups[k - 1] + s * s
                now = nxt
                S[x, r:r + 8, :] += 3.0 * groups[0] + 2.0 * groups[1] + groups[2]

    def mass(index, total):
        out = jnp.zeros(index.shape, f32)
        for s in range(-3, 4):
            ok = (index + s >= 0) & (index + s < total)
            out = out + jnp.where(ok, 4.0 - abs(s), 0.0)
        return out

    mz = mass(my_z * Z + lane, nz * Z)
    for r in chunks:
        my = mass(my_y * R + (r - LO) + sub, ny * R)
        inv_yz = (-3.0 * (1.0 - FLOOR) / (48.0 * L)) / (my * mz)
        vs = []
        for x in range(X):
            density = (seed[x, r - LO:r - LO + 8, :].astype(f32) + 1.0) / 16.0
            mx = float(sum(4 - abs(s) for s in range(-3, 4) if 0 <= x + s < X))
            vs.append(S[x, r:r + 8, :] * (density * density) * inv_yz * (1.0 / mx))
        b = zero
        for x in range(X):
            v = 4.0 * vs[x]
            for s in (1, 2, 3):
                for o in (x - s, x + s):
                    if 0 <= o < X:
                        v = v + (4.0 - s) * vs[o]
            S[x, r:r + 8, :] = v
            b = jnp.where(lane >= 16 * x, roll(v, 16 * x + 8), b)
        PZ[r - LO:r - LO + 8, :] = b

    top, bottom = pl.ds(R - 8, 8), pl.ds(0, 8)
    final = (
        (1, 0, S.at[:, last], SLO), (-1, 0, S.at[:, first], SHI),
        (0, 1, PZ, PZL.at[mid]), (0, -1, PZ, PZH.at[mid]),
        (1, 1, PZ.at[top], PZL.at[low]), (1, -1, PZ.at[top], PZH.at[low]),
        (-1, 1, PZ.at[bottom], PZL.at[high]), (-1, -1, PZ.at[bottom], PZH.at[high]),
    )
    exchange(STEPS + 1, final, True)
    exchange(STEPS + 1, final, False)
    for x in range(X):
        S[x, 0:LO, :] = SLO[x]
        S[x, HI:RP, :] = SHI[x]
    for r in (0,) + chunks + (HI,):
        PM[r:r + 8, :] = jnp.where(lane16 < 8, PZL[r:r + 8, :], PZH[r:r + 8, :])

    def along_y(get):
        v = 4.0 * get(0)
        for s in (1, 2, 3):
            v = v + (4.0 - s) * (get(s) + get(-s))
        return v

    for r in chunks:
        pm = along_y(lambda s: PM[r + s:r + s + 8, :])
        for x in range(X):
            v = along_y(lambda s: S[x, r + s:r + s + 8, :])
            w = roll(pm, -(16 * x + 8))
            out = 4.0 * v
            for s in (1, 2, 3):
                up = jnp.where(lane >= 128 - s, roll(w, -s), roll(v, -s))
                down = jnp.where(lane < s, roll(w, s), roll(v, s))
                out = out + (4.0 - s) * (up + down)
            sens[x, r - LO:r - LO + 8, :] = out


def on_device(ny, nz, seed, heat, source, fixed):
    f32 = jnp.float32
    v = pltpu.VMEM
    scratch = [
        v((STEPS, L, X, RP, Z), f32),
        v((STEPS, RP, Z), f32), v((STEPS, RP, Z), f32), v((STEPS, RP, Z), f32),
        v((STEPS, L, X, Z), f32), v((STEPS, L, X, Z), f32),
        v((STEPS, L, X, Z), f32), v((STEPS, L, X, Z), f32),
        v((STEPS, RP, Z), f32), v((1, RP, Z), f32),
        v((X, RP, Z), f32), v((X, RP, Z), f32), v((X, RP, Z), f32),
        v((X, R, Z), f32), v((X, R, Z), f32),
        v((2, X, RP, Z), f32),
        v((2 * STEPS, L, 8, Z), f32), v((8, Z), f32), v((STEPS, L, 8, Z), f32),
        v((R, Z), f32), v((RP, Z), f32), v((X, Z), f32), v((X, Z), f32),
        v((X, RP, Z), f32), v((X, 8, Z), f32), v((X, 8, Z), f32),
        v((R, Z), f32), v((RP, Z), f32), v((RP, Z), f32), v((RP, Z), f32),
        v((nz, 8, Z), f32), v((ny, 8, Z), f32),
        pltpu.SemaphoreType.DMA((STEPS + 2, 10)), pltpu.SemaphoreType.DMA((STEPS + 2, 10)),
        pltpu.SemaphoreType.DMA((ny + nz,)), pltpu.SemaphoreType.DMA((ny + nz,)),
    ]
    return pl.pallas_call(
        functools.partial(kernel, ny, nz),
        out_shape=(jax.ShapeDtypeStruct((L, X, R, Z), f32), jax.ShapeDtypeStruct((X, R, Z), f32)),
        in_specs=[pl.BlockSpec(memory_space=pltpu.VMEM)] * 4,
        out_specs=(pl.BlockSpec(memory_space=pltpu.VMEM),) * 2,
        scratch_shapes=scratch,
        compiler_params=pltpu.CompilerParams(
            collective_id=0, has_side_effects=True, vmem_limit_bytes=40 * 2**20
        ),
    )(seed, heat, source, fixed)


def solution(mesh):
    in_specs = (
        P(None, "gy", "gz"),
        P(None, None, "gy", "gz"),
        P(None, "gy", "gz"),
        P(None, "gy", "gz"),
    )
    out_specs = (P(None, None, "gy", "gz"), P(None, "gy", "gz"))
    body = functools.partial(on_device, mesh.shape["gy"], mesh.shape["gz"])
    return jax.shard_map(body, mesh=mesh, in_specs=in_specs, out_specs=out_specs, check_vma=False)
```

time: 727 us -> 219 us (0.30); the launches traced: 716 us -> 218 us
  blocking collectives: 283 us -> 0 us
  other arithmetic: 254 us -> 0 us
  Pallas kernels: 0 us -> 211 us
  local copies, waits for them, and re-layouts: 76.2 us -> 6.46 us
  starting transfers between devices: 69.7 us -> 0 us
  waiting for transfers between devices: 32.1 us -> 0 us
    psum x7 -> x0, blocking collectives: 283 us -> none  [the longest x4 160 us: search_total(): return column(lax.psum(inner_sum(residual_now, precond_now), ('gy', 'gz')))]
    pallas_call x0 -> x1, Pallas kernels: none -> 211 us  [on_device(): pl.pallas_call(functools.partial(kernel, ny, nz), out_shape=(jax.ShapeDty...]
    reduce_sum x8 -> x0, other arithmetic: 179 us -> none  [the longest x7 169 us: inner_sum(): return jnp.sum(left * right, axis=(1, 2, 3))]
    ppermute x26 -> x0, starting transfers between devices: 69.7 us -> none  [the longest x12 48 us: padded_2(): lax.ppermute(lax.slice_in_dim(block, block.shape[dim] - width, None, axis...]
    concatenate x14 -> x0, other arithmetic: 50.4 us -> none  [the longest x12 50 us: padded_2(): block = jnp.concatenate([low, block, high], axis=dim)]
    slice x30 -> x0, local copies, waits for them, and re-layouts: 46 us -> none  [the longest x17 25.8 us: padded_2(): lax.slice_in_dim(block, block.shape[dim] - width, None, axis=dim)]
    ppermute x26 -> x0, waiting for transfers between devices: 32.1 us -> none  [the longest x12 28.1 us: padded_2(): lax.ppermute(lax.slice_in_dim(block, 0, width, axis=dim), axis, backward)]
    ppermute x10 -> x0, local copies, waits for them, and re-layouts: 25.3 us -> none  [the longest x5 14.1 us: padded_2(): lax.ppermute(lax.slice_in_dim(block, block.shape[dim] - width, None, axis...]
  transfers between devices with their start and end apart: 26 -> 0, of which waited for: 15 -> 0; matrix products, arithmetic and copies ran while one was open for 5% -> 0% of each run, Pallas kernels for 0% -> 0%
where the time goes in v1:
time: 219 us; the launch traced here: 218 us
  Pallas kernels  211 us (96%)
  local copies, waits for them, and re-layouts  6.46 us (3%)
    pallas_call x1, Pallas kernels, on_device(): pl.pallas_call(functools.partial(kernel, ny, nz), out_shape=(jax.ShapeDty...  211 us
    unnamed x10, local copies, waits for them, and re-layouts  6.46 us

profile of v1, /device:TPU:0, one launch (start us, length us, event | category | flops | bytes accessed | tf_op | source)
XLA Modules:
  0.0 218.5 jit_solution(6590689245484498090)
XLA Ops:
  0.6 0.0 copy-start
  0.6 1.6 copy-done
  2.2 0.0 copy-start.1
  2.2 0.9 copy-done.1
  3.2 0.0 copy-start.2
  3.2 0.9 copy-done.2
  4.1 0.0 copy-start.3
  4.1 0.9 copy-done.3
  5.1 211.4 %shard_map.59 = (f32[8,8,64,128]{3,2,1,0:T(8,128)S(1)}, f32[8,64,128]{2,1,0:T(8,128)S(1)}) custom-call(s32[8,64,128]{2,1,0:T(8,128)S(1)} %copy-done.1, f32[8,8,64,128]{3,2,1,0:T(8,128)S(1)} %copy-done, s32[8,64,128]{2,1,0:T(8,128)S(1)} %copy-done.2, s32[8,64,128]{2,1,0:T(8,128)S(1)} %copy-done.3), custom_call_target="tpu_custom_call" | custom-call | tf_op jit(solution)/shard_map/pallas_call | solution.py:486
  216.4 1.3 copy.8
  217.8 0.7 copy.9
Async XLA Ops:
  0.6 1.6 copy-start
  2.2 0.9 copy-start.1
  3.2 0.9 copy-start.2
  4.1 0.9 copy-start.3

commit v2 on v1

--- a/solution.py
+++ b/solution.py
@@ -27,12 +27,13 @@
 
 
 def kernel(ny, nz, seed, heat, source, fixed, temp, sens,
-           U, BL, BO, BH, ELO, EHI, ETOP, EBOT, W, WC,
+           U0, U1, U2, U3, BL, BO, BH, ELO, EHI, ETOP, EBOT, W, WC,
            C1, C2, C3, INV, DIAG, PS, ACC, RED, COEF,
            BC, BCL, CTOP, CLO, S, SLO, SHI, PZ, PZL, PZH, PM,
            AZ, AY, send, recv, rsend, rrecv):
     my_y, my_z = lax.axis_index("gy"), lax.axis_index("gz")
     f32 = jnp.float32
+    U = (U0, U1, U2, U3)
     lane = lax.broadcasted_iota(jnp.int32, (8, Z), 1)
     sub = lax.broadcasted_iota(jnp.int32, (8, Z), 0)
     lane16 = lax.rem(lane, 16)
@@ -161,7 +162,7 @@
                 inv = INV[x, q:q + 8, :]
                 rhs = heat[l, x, q:q + 8, :] * source[x, q:q + 8, :].astype(f32)
                 v = rhs * inv
-                U[0, l, x, r:r + 8, :] = v
+                U[0][l, x, r:r + 8, :] = v
                 acc = acc + v * v * DIAG[x, q:q + 8, :]
                 b = jnp.where(lane16 >= 2 * x, roll(v, 16 * l + 2 * x + 1), b)
                 edges(0, l, x, r, v)
@@ -173,8 +174,8 @@
         @pl.loop(0, L)
         def _(l):
             for x in range(X):
-                U[j, l, x, LO - 1:LO, :] = ELO[j, l, x:x + 1, :]
-                U[j, l, x, HI:HI + 1, :] = EHI[j, l, x:x + 1, :]
+                U[j][l, x, LO - 1:LO, :] = ELO[j, l, x:x + 1, :]
+                U[j][l, x, HI:HI + 1, :] = EHI[j, l, x:x + 1, :]
 
         def up_x(v):
             return jnp.where(lane16 < 14, roll(v, -2), 0.0)
@@ -209,32 +210,39 @@
             W[j, r:r + 8, :] = jnp.where(lax.rem(lane, 2) == 0, roll(BH[j, r:r + 8, :], -1), push)
         W[j, HI:RP, :] = roll(BH[j, HI:RP, :], -1)
 
+    def next_row(v, following):
+        return pltpu.roll(jnp.where(sub == 0, following, v), 7, 0)
+
     def step(j):
         scale = 2.0 if j else 1.0
 
         @pl.loop(0, L)
         def _(l):
             back = 128 - (16 * l + 1)
-            acc_a, acc_b = zero, zero
-            for r in (0,) + chunks:
-                w0, w1 = W[j, r:r + 8, :], W[j, r + 1:r + 9, :]
+            def chunk(r, above, sums):
+                here, ahead = pl.ds(r, 8), pl.ds(r + 8, 8)
+                if sums is not None:
+                    here, ahead = pl.ds(pl.multiple_of(r, 8), 8), pl.ds(pl.multiple_of(r + 8, 8), 8)
+                    owned = pl.ds(pl.multiple_of(r - LO, 8), 8)
+                    acc_a, acc_b = sums
+                w0 = W[j, here, :]
+                w1 = next_row(w0, W[j, ahead, :])
                 ws, wd = w0 + w1, w1 - w0
-                b = zero
-                carry = None
-                last_f = None
 
                 def node(x):
-                    u0, u1 = U[j, l, x, r:r + 8, :], U[j, l, x, r + 1:r + 9, :]
+                    u0 = U[j][l, x, here, :]
+                    u1 = next_row(u0, U[j][l, x, ahead, :])
                     amount = back - 2 * x
                     ys, yd = u0 + u1, u1 - u0
                     ns = jnp.where(lane == 127, roll(ws, amount), roll(ys, 127))
                     nd = jnp.where(lane == 127, roll(wd, amount), roll(yd, 127))
                     return (ys + ns, yd + nd, ns - ys, nd - yd)
 
-                now = node(0)
+                now, carry, b = node(0), None, zero
+                pushed, news = [], []
                 for x in range(X):
                     nxt = node(x + 1) if x + 1 < X else None
-                    cs = (C1[x, r:r + 8, :], C2[x, r:r + 8, :], C3[x, r:r + 8, :])
+                    cs = (C1[x, here, :], C2[x, here, :], C3[x, here, :])
                     outs, new_carry = [], []
                     for i, k in enumerate((0, 1, 1, 2)):
                         f = now[i]
@@ -255,31 +263,40 @@
                     carry = new_carry
                     now = nxt
                     ss, sd, ds, dd = outs
-                    PS[0, x, r:r + 8, :] = ss + sd
-                    PS[1, x, r:r + 8, :] = ds + dd
-                    if r == 0:
+                    ps, pd = ss + sd, ds + dd
+                    pushed += [ps, pd]
+                    if sums is None:
                         continue
-                    q = r - LO
-                    es = ss - sd + PS[0, x, r - 1:r + 7, :]
-                    ed = ds - dd + PS[1, x, r - 1:r + 7, :]
+                    es = ss - sd + pltpu.roll(jnp.where(sub == 7, above[2 * x], ps), 1, 0)
+                    ed = ds - dd + pltpu.roll(jnp.where(sub == 7, above[2 * x + 1], pd), 1, 0)
                     push = jnp.where(lane == 0, roll(w0, back - 2 * x), roll(es + ed, 1))
                     image = es - ed + push
-                    v = U[j, l, x, r:r + 8, :]
-                    new = image * (INV[x, q:q + 8, :] * (scale / HALF)) - scale * v
+                    v = U[j][l, x, here, :]
+                    new = image * (INV[x, owned, :] * (scale / HALF)) - scale * v
                     if j:
-                        new = new - U[j - 1, l, x, r:r + 8, :]
-                    weighted = new * DIAG[x, q:q + 8, :]
+                        new = new - U[j - 1][l, x, here, :]
+                    weighted = new * DIAG[x, owned, :]
                     acc_a = acc_a + v * weighted
                     if j + 1 < STEPS:
                         acc_b = acc_b + new * weighted
-                        U[j + 1, l, x, r:r + 8, :] = new
                         b = jnp.where(lane16 >= 2 * x, roll(new, 16 * l + 2 * x + 1), b)
-                        edges(j + 1, l, x, r, new)
-                if r and j + 1 < STEPS:
-                    pack_tail(j + 1, l, r, b)
+                        news.append(new)
+                if news:
+                    for x, new in enumerate(news):
+                        U[j + 1][l, x, here, :] = new
+                    BO[j + 1, here, :] = jnp.where(group == l, b, BO[j + 1, here, :])
+                if sums is None:
+                    return tuple(pushed)
+                return tuple(pushed), (acc_a, acc_b)
+
+            _, (acc_a, acc_b) = lax.fori_loop(
+                1, HI // 8, lambda c, carry: chunk(c * 8, *carry), (chunk(0, None, None), (zero, zero)))
             ACC[2 * j + 1, l] = acc_a
             if j + 1 < STEPS:
                 ACC[2 * j + 2, l] = acc_b
+                for x in range(X):
+                    EBOT[j + 1, l, x:x + 1, :] = U[j + 1][l, x, LO:LO + 1, :]
+                    ETOP[j + 1, l, x:x + 1, :] = U[j + 1][l, x, HI - 1:HI, :]
 
     for j in range(STEPS):
         exchange(j, halo(j), False)
@@ -371,9 +388,9 @@
         back = 128 - (16 * l + 1)
         for x in range(X):
             for r in chunks + (HI,):
-                t = cs[0] * U[0, l, x, r:r + 8, :]
+                t = cs[0] * U[0][l, x, r:r + 8, :]
                 for i in range(1, STEPS):
-                    t = t + cs[i] * U[i, l, x, r:r + 8, :]
+                    t = t + cs[i] * U[i][l, x, r:r + 8, :]
                 PS[0, x, r:r + 8, :] = t
                 if r < HI:
                     temp[l, x, r - LO:r - LO + 8, :] = t
@@ -467,14 +484,14 @@
     f32 = jnp.float32
     v = pltpu.VMEM
     scratch = [
-        v((STEPS, L, X, RP, Z), f32),
+        *(v((L, X, RP, Z), f32) for _ in range(STEPS)),
         v((STEPS, RP, Z), f32), v((STEPS, RP, Z), f32), v((STEPS, RP, Z), f32),
         v((STEPS, L, X, Z), f32), v((STEPS, L, X, Z), f32),
         v((STEPS, L, X, Z), f32), v((STEPS, L, X, Z), f32),
         v((STEPS, RP, Z), f32), v((1, RP, Z), f32),
         v((X, RP, Z), f32), v((X, RP, Z), f32), v((X, RP, Z), f32),
         v((X, R, Z), f32), v((X, R, Z), f32),
-        v((2, X, RP, Z), f32),
+        v((1, X, RP, Z), f32),
         v((2 * STEPS, L, 8, Z), f32), v((8, Z), f32), v((STEPS, L, 8, Z), f32),
         v((R, Z), f32), v((RP, Z), f32), v((X, Z), f32), v((X, Z), f32),
         v((X, RP, Z), f32), v((X, 8, Z), f32), v((X, 8, Z), f32),

time: 219 us -> 122 us (0.56)
  Pallas kernels: 211 us -> 115 us
    pallas_call x1, Pallas kernels: 211 us -> 115 us  [on_device(): pl.pallas_call(functools.partial(kernel, ny, nz), out_shape=(jax.ShapeDty...]
where the time goes in v2:
time: 122 us
  Pallas kernels  115 us (94%)
  local copies, waits for them, and re-layouts  6.46 us (5%)
    pallas_call x1, Pallas kernels, on_device(): pl.pallas_call(functools.partial(kernel, ny, nz), out_shape=(jax.ShapeDty...  115 us
    unnamed x10, local copies, waits for them, and re-layouts  6.46 us

profile of v2, /device:TPU:0, one launch (start us, length us, event | category | flops | bytes accessed | tf_op | source)
XLA Modules:
  0.0 121.7 jit_solution(14174153652682564401)
XLA Ops:
  0.6 0.0 copy-start
  0.6 1.6 %copy-done = f32[8,8,64,128]{3,2,1,0:T(8,128)S(1)} copy-done((f32[8,8,64,128]{3,2,1,0:T(8,128)S(1)}, f32[8,8,64,128]{3,2,1,0:T(8,128)}, u32[]{:S(2)}) %copy-start) | copy-done | bytes 2097176
  2.2 0.0 copy-start.1
  2.2 0.9 copy-done.1
  3.2 0.0 copy-start.2
  3.2 0.9 copy-done.2
  4.1 0.0 copy-start.3
  4.1 0.9 copy-done.3
  5.1 114.6 %shard_map.59 = (f32[8,8,64,128]{3,2,1,0:T(8,128)S(1)}, f32[8,64,128]{2,1,0:T(8,128)S(1)}) custom-call(s32[8,64,128]{2,1,0:T(8,128)S(1)} %copy-done.1, f32[8,8,64,128]{3,2,1,0:T(8,128)S(1)} %copy-done, s32[8,64,128]{2,1,0:T(8,128)S(1)} %copy-done.2, s32[8,64,128]{2,1,0:T(8,128)S(1)} %copy-done.3), custom_call_target="tpu_custom_call" | custom-call | tf_op jit(solution)/shard_map/pallas_call | solution.py:503
  119.7 1.3 %copy.8 = f32[8,8,64,128]{3,2,1,0:T(8,128)} copy(f32[8,8,64,128]{3,2,1,0:T(8,128)S(1)} %get-tuple-element.4) | data formatting | bytes 4194304
  121.0 0.7 copy.9
Async XLA Ops:
  0.6 1.6 %copy-start = (f32[8,8,64,128]{3,2,1,0:T(8,128)S(1)}, f32[8,8,64,128]{3,2,1,0:T(8,128)}, u32[]{:S(2)}) copy-start(f32[8,8,64,128]{3,2,1,0:T(8,128)} %heat.1) | copy-start | bytes 6291460
  2.2 0.9 copy-start.1
  3.2 0.9 copy-start.2
  4.1 0.9 copy-start.3

commit v3 on v2

--- a/solution.py
+++ b/solution.py
@@ -290,7 +290,7 @@
                 return tuple(pushed), (acc_a, acc_b)
 
             _, (acc_a, acc_b) = lax.fori_loop(
-                1, HI // 8, lambda c, carry: chunk(c * 8, *carry), (chunk(0, None, None), (zero, zero)))
+                1, HI // 8, lambda c, carry: chunk(c * 8, *carry), (chunk(0, None, None), (zero, zero)), unroll=2)
             ACC[2 * j + 1, l] = acc_a
             if j + 1 < STEPS:
                 ACC[2 * j + 2, l] = acc_b

time: 122 us -> 96 us (0.79)
  Pallas kernels: 115 us -> 88.7 us
    pallas_call x1, Pallas kernels: 115 us -> 88.7 us  [on_device(): pl.pallas_call(functools.partial(kernel, ny, nz), out_shape=(jax.ShapeDty...]
where the time goes in v3:
time: 96 us; the launch traced here: 95.8 us
  Pallas kernels  88.7 us (92%)
  local copies, waits for them, and re-layouts  6.46 us (7%)
    pallas_call x1, Pallas kernels, on_device(): pl.pallas_call(functools.partial(kernel, ny, nz), out_shape=(jax.ShapeDty...  88.7 us
    unnamed x10, local copies, waits for them, and re-layouts  6.46 us

profile of v3, /device:TPU:0, one launch (start us, length us, event | category | flops | bytes accessed | tf_op | source)
XLA Modules:
  0.0 95.8 jit_solution(17675356285579437112)
XLA Ops:
  0.6 0.0 copy-start
  0.6 1.6 %copy-done = f32[8,8,64,128]{3,2,1,0:T(8,128)S(1)} copy-done((f32[8,8,64,128]{3,2,1,0:T(8,128)S(1)}, f32[8,8,64,128]{3,2,1,0:T(8,128)}, u32[]{:S(2)}) %copy-start) | copy-done | bytes 2097176
  2.2 0.0 copy-start.1
  2.2 0.9 copy-done.1
  3.2 0.0 copy-start.2
  3.2 0.9 copy-done.2
  4.1 0.0 copy-start.3
  4.1 0.9 copy-done.3
  5.1 88.7 %shard_map.59 = (f32[8,8,64,128]{3,2,1,0:T(8,128)S(1)}, f32[8,64,128]{2,1,0:T(8,128)S(1)}) custom-call(s32[8,64,128]{2,1,0:T(8,128)S(1)} %copy-done.1, f32[8,8,64,128]{3,2,1,0:T(8,128)S(1)} %copy-done, s32[8,64,128]{2,1,0:T(8,128)S(1)} %copy-done.2, s32[8,64,128]{2,1,0:T(8,128)S(1)} %copy-done.3), custom_call_target="tpu_custom_call" | custom-call | tf_op jit(solution)/shard_map/pallas_call | solution.py:503
  93.8 1.3 %copy.8 = f32[8,8,64,128]{3,2,1,0:T(8,128)} copy(f32[8,8,64,128]{3,2,1,0:T(8,128)S(1)} %get-tuple-element.4) | data formatting | bytes 4194304
  95.1 0.7 copy.9
Async XLA Ops:
  0.6 1.6 %copy-start = (f32[8,8,64,128]{3,2,1,0:T(8,128)S(1)}, f32[8,8,64,128]{3,2,1,0:T(8,128)}, u32[]{:S(2)}) copy-start(f32[8,8,64,128]{3,2,1,0:T(8,128)} %heat.1) | copy-start | bytes 6291460
  2.2 0.9 copy-start.1
  3.2 0.9 copy-start.2
  4.1 0.9 copy-start.3
